TPU v7x, 256 devices: a whole 4x4x8 slice. The times are simulated.
256 devices in a mesh: spec: 32 (over y, x, z_hi), pix: 8 (over z_lo, core).
Axes of the slice: x: 4, y: 4, z: 8 (z_hi: 2, z_lo: 4; z = z_hi * 4 + z_lo), core: 2. Of those that a mesh axis runs over, the one named last changes fastest.
Arguments:
- spectra: float32 [2, 16, 4096, 2048], P(None, None, 'pix', 'spec'), may hold values from -6 to 6
- dispersion: float32 [2048], replicated, may hold values from -3.140625 to 3.140625
- window_start: int32 [32], replicated, may hold values from -4 to 248, as said below
- window_width: int32 [32], replicated, may hold values from 8 to 16, as said below
- pupil: float32 [2, 2048, 4096], P(None, None, 'pix'), may hold values from -0.0625 to 0.0625
Outputs:
- focused: float32 [32, 16, 2048], P('spec', None, 'pix')
Inputs may be any that keep to these rules, and one draw needn't show every extreme that they name: window_start[d] lies between d * 8 - 4 and d * 8; the first owner's window starts at -4 and the last owner's at 248. window_start[d] + window_width[d] lies between (d + 1) * 8 and (d + 1) * 8 + 4.
All inputs are finite; a program needn't handle non-finite values.
Results may differ from a plain program's by a relative error of at most 0.000067.
Values sent between devices are 32-bit elements; how exact they have to be, the bound alone decides.
A program may use at most 128 MiB of HBM per device.

v0:
```python
import math

import jax
import jax.numpy as jnp
from jax import lax
from jax.experimental import pallas as pl
from jax.experimental.pallas import tpu as pltpu
from jax.sharding import PartitionSpec as P

K = 2048
MESH = pl.DeviceIdType.MESH
F32 = jnp.float32
BF16 = jnp.bfloat16
ROUNDS = 4
STEP = 2.0 * math.pi / K
NT = (((1,), (1,)), ((), ()))


def split(values):
    high = values.astype(BF16)
    return high, (values - high.astype(F32)).astype(BF16)


def kernel(
    spectra, disp, start, width, pupil, out,
    xbuf, xhl, th, tl, cosa, sina, cosb, sinb, pstage, ph, plo,
    part, zrecv, gsend, grecv, abuf, csend, own, crecv, frecv, hsend, hrecv,
    xs, xr, zs, zr, gs, gr, cs, cr, fs, fr, hs, hr, ps,
):
    s = lax.axis_index("spec")
    p = lax.axis_index("pix")
    me = s // 2
    zh = s % 2
    y = me // 4
    x = me % 4
    zl = p // 2
    co = p % 2
    partner = {"spec": s + 1 - 2 * zh}
    sibling = {"pix": zl * 2 + 1 - co}
    before = {"spec": (s + 31) % 32}
    after = {"spec": (s + 1) % 32}

    def peer(t):
        return ((y + t // 4) % 4) * 4 + (x + t % 4) % 4

    def along(dz):
        return (zl + dz) % 4

    barrier = pltpu.get_barrier_semaphore()

    def greet(t, carry):
        pl.semaphore_signal(
            barrier, inc=1, device_id={"spec": peer(t) * 2 + zh}, device_id_type=MESH
        )
        return carry

    lax.fori_loop(1, 16, greet, 0)
    for device in (partner, sibling, before, after):
        pl.semaphore_signal(barrier, inc=1, device_id=device, device_id_type=MESH)
    for dz in (1, 2, 3):
        pl.semaphore_signal(
            barrier, inc=1, device_id={"pix": along(dz) * 2 + co}, device_id_type=MESH
        )
    pl.semaphore_wait(barrier, 22)

    def block(r, j):
        return spectra.at[
            :, r * 4 + j // 4, :, pl.ds(pl.multiple_of((j % 4) * 128, 128), 128)
        ]

    def send_round(r, carry):
        def send(t, inner):
            j = peer(t)
            pltpu.make_async_remote_copy(
                src_ref=block(r, j), dst_ref=xbuf.at[r, me], send_sem=xs.at[0],
                recv_sem=xr.at[r], device_id={"spec": j * 2 + zh}, device_id_type=MESH,
            ).start()
            return inner

        lax.fori_loop(1, 16, send, 0)
        pltpu.make_async_copy(block(r, me), xbuf.at[r, me], xr.at[r]).start()
        return carry

    lax.fori_loop(0, ROUNDS, send_round, 0)

    def fetch(n, slot):
        return pltpu.make_async_copy(
            pupil.at[n // 4, pl.ds((n % 4) * 512, 512)], pstage.at[slot], ps.at[slot]
        )

    fetch(0, 0).start()

    lane = lax.broadcasted_iota(jnp.int32, (8, K), 1)
    cin = (lane // 64) % 2
    wave = (lane // 128) * 128 + zh * 64 + lane % 64
    phase = jnp.broadcast_to(disp[...], (8, K))
    up = pltpu.roll(phase, 64, 1)
    down = pltpu.roll(phase, K - 64, 1)
    phase = jnp.where(cin == zh, phase, jnp.where(cin == 1, up, down))
    fine = lax.broadcasted_iota(jnp.int32, (8, K), 0)
    beta = STEP * ((fine * wave - cin * 512) & (K - 1)).astype(F32) + phase
    scale = 1.0 / math.sqrt(K)
    cosb[...] = jnp.cos(beta) * scale
    sinb[...] = jnp.sin(beta) * scale

    def coarse(n, carry):
        row = lax.broadcasted_iota(jnp.int32, (8, K), 0) + n * 8
        zg = jnp.where(row < 16, 1 - zh, zh)
        q = (row % 16) * 2 + zg
        alpha = STEP * ((8 * q * wave) & (K - 1)).astype(F32)
        cosa[pl.ds(pl.multiple_of(n * 8, 8), 8), :] = jnp.cos(alpha)
        sina[pl.ds(pl.multiple_of(n * 8, 8), 8), :] = jnp.sin(alpha)
        return carry

    lax.fori_loop(0, 4, coarse, 0)

    def rows(n, carry):
        ca = cosa[pl.ds(n, 1), :]
        sa = sina[pl.ds(n, 1), :]
        real = ca * cosb[...] - sa * sinb[...]
        imag = -(sa * cosb[...] + ca * sinb[...])
        high, low = split(jnp.concatenate([real, imag], axis=0))
        at = pl.ds(pl.multiple_of(n * 16, 16), 16)
        th[at, :] = high
        tl[at, :] = low
        return carry

    lax.fori_loop(0, 32, rows, 0)

    def convert(n, carry):
        slot = n % 2

        @pl.when(n < 7)
        def _():
            fetch(n + 1, 1 - slot).start()

        fetch(n, slot).wait()

        def piece(m, inner):
            high, low = split(pstage[slot, pl.ds(pl.multiple_of(m * 64, 64), 64), :])
            at = pl.ds(pl.multiple_of((n % 4) * 512 + m * 64, 64), 64)
            ph[n // 4, at, :] = high
            plo[n // 4, at, :] = low
            return inner

        lax.fori_loop(0, 8, piece, 0)
        return carry

    lax.fori_loop(0, 8, convert, 0)

    def await_all(ref, sem):
        pltpu.make_async_copy(ref, ref, sem).wait()

    def half_copy(r):
        return pltpu.make_async_remote_copy(
            src_ref=part.at[r, 0], dst_ref=zrecv.at[r], send_sem=zs.at[r],
            recv_sem=zr.at[r], device_id=partner, device_id_type=MESH,
        )

    def core_copy(r):
        return pltpu.make_async_remote_copy(
            src_ref=csend.at[r], dst_ref=crecv.at[r], send_sem=cs.at[r],
            recv_sem=cr.at[r], device_id=sibling, device_id_type=MESH,
        )

    def transform(r):
        await_all(xbuf.at[r], xr.at[r])

        def piece(n, carry):
            high, low = split(xbuf[r, n].reshape(128, 128))
            at = pl.ds(pl.multiple_of(n * 128, 128), 128)
            xhl[at, 0:128] = high
            xhl[at, 128:256] = low
            return carry

        lax.fori_loop(0, 16, piece, 0)
        for half in (0, 1):
            at = slice(half * 256, half * 256 + 256)
            both = jnp.dot(th[at, :], xhl[...], preferred_element_type=F32)
            rest = jnp.dot(tl[at, :], xhl[:, 0:128], preferred_element_type=F32)
            part[r, half] = both[:, 0:128] + (both[:, 128:256] + rest)
            if half == 0:
                half_copy(r).start()

    def hand_out(r):
        half_copy(r).wait_recv()
        gsend[r] = (part[r, 1] + zrecv[r]).reshape(16, 16, 128)

        def send(t, carry):
            j = peer(t)
            pltpu.make_async_remote_copy(
                src_ref=gsend.at[r, j], dst_ref=grecv.at[r, me], send_sem=gs.at[0],
                recv_sem=gr.at[r], device_id={"spec": j * 2 + zh}, device_id_type=MESH,
            ).start()
            return carry

        lax.fori_loop(1, 16, send, 0)
        pltpu.make_async_copy(gsend.at[r, me], grecv.at[r, me], gr.at[r]).start()

    def project(r):
        await_all(grecv.at[r], gr.at[r])
        for i in range(4):
            real = jnp.concatenate([grecv[r, i * 4 + b, 0:8, :] for b in range(4)], axis=1)
            imag = jnp.concatenate([grecv[r, i * 4 + b, 8:16, :] for b in range(4)], axis=1)
            abuf[i * 8 : i * 8 + 8, 0:512] = real
            abuf[i * 8 : i * 8 + 8, 512:1024] = -imag
            abuf[32 + i * 8 : 40 + i * 8, 0:512] = imag
            abuf[32 + i * 8 : 40 + i * 8, 512:1024] = real
        high, low = split(abuf[...])
        stack = jnp.concatenate([high, low], axis=0)

        def product(b, core):
            at = pl.ds(pl.multiple_of((b * 2 + core) * 256, 256), 256)
            both = lax.dot_general(
                stack[:, 0:512], ph[0, at, :], NT, preferred_element_type=F32
            ) + lax.dot_general(stack[:, 512:1024], ph[1, at, :], NT, preferred_element_type=F32)
            rest = lax.dot_general(
                high[:, 0:512], plo[0, at, :], NT, preferred_element_type=F32
            ) + lax.dot_general(high[:, 512:1024], plo[1, at, :], NT, preferred_element_type=F32)
            return both[0:64] + (both[64:128] + rest)

        for b in range(4):
            csend[r, b] = product(b, 1 - co)
        core_copy(r).start()
        for b in range(4):
            own[r, b] = product(b, co)

    def along_copy(r, dz):
        return pltpu.make_async_remote_copy(
            src_ref=own.at[r, along(dz)], dst_ref=frecv.at[r, dz - 1], send_sem=fs.at[r, dz - 1],
            recv_sem=fr.at[r, dz - 1], device_id={"pix": along(dz) * 2 + co}, device_id_type=MESH,
        )

    def combine(r):
        core_copy(r).wait_recv()
        own[r] = own[r] + crecv[r]
        for dz in (1, 2, 3):
            along_copy(r, dz).start()

    gate = s * 8 + lax.broadcasted_iota(jnp.int32, (8, 256), 0)

    def weight(owner):
        first = start[owner]
        return ((gate >= first) & (gate < first + width[owner])).astype(F32)

    def finish(r):
        for dz in (1, 2, 3):
            along_copy(r, dz).wait_recv()
        total = own[r, zl] + (frecv[r, 0] + (frecv[r, 1] + frecv[r, 2]))
        power = total[0:32] * total[0:32] + total[32:64] * total[32:64]
        for n, owner in enumerate((s, (s + 31) % 32, (s + 1) % 32)):
            w = weight(owner)
            for i in range(4):
                hsend[n, r, i : i + 1, :] = jnp.sum(
                    power[i * 8 : i * 8 + 8] * w, axis=0, keepdims=True
                )

    def turn(n, carry):
        pl.when(n < 4)(lambda: transform(n))

        @pl.when((n >= 1) & (n < 4))
        def _():
            project(n - 1)
            combine(n - 1)

        pl.when((n >= 2) & (n < 5))(lambda: finish(n - 2))
        pl.when(n < 4)(lambda: hand_out(n))

        @pl.when(n == 4)
        def _():
            project(n - 1)
            combine(n - 1)
            finish(n - 1)

        return carry

    lax.fori_loop(0, 5, turn, 0)

    copies = []
    for n, device in ((1, before), (2, after)):
        copy = pltpu.make_async_remote_copy(
            src_ref=hsend.at[n], dst_ref=hrecv.at[n - 1], send_sem=hs.at[n - 1],
            recv_sem=hr.at[n - 1], device_id=device, device_id_type=MESH,
        )
        copy.start()
        copies.append(copy)

    def sent(r, carry):
        await_all(xbuf.at[r, pl.ds(0, 15)], xs.at[0])
        await_all(gsend.at[r, pl.ds(0, 15)], gs.at[0])
        half_copy(r).wait_send()
        core_copy(r).wait_send()
        for dz in (1, 2, 3):
            along_copy(r, dz).wait_send()
        return carry

    lax.fori_loop(0, ROUNDS, sent, 0)
    for copy in copies:
        copy.wait()
    for r in range(ROUNDS):
        out[r * 4 : r * 4 + 4, :] = hsend[0, r] + (hrecv[0, r] + hrecv[1, r])


def local(spectra, dispersion, window_start, window_width, pupil):
    vmem = pltpu.VMEM
    dma = pltpu.SemaphoreType.DMA
    hbm = pl.BlockSpec(memory_space=pl.ANY)
    smem = pl.BlockSpec(memory_space=pltpu.SMEM)
    focused = pl.pallas_call(
        kernel,
        out_shape=jax.ShapeDtypeStruct((16, 256), F32),
        in_specs=[hbm, pl.BlockSpec(memory_space=pltpu.VMEM), smem, smem, hbm],
        out_specs=pl.BlockSpec(memory_space=pltpu.VMEM),
        scratch_shapes=[
            vmem((4, 16, 2, 64, 128), F32),
            vmem((K, 256), BF16),
            vmem((512, K), BF16),
            vmem((512, K), BF16),
            vmem((32, K), F32),
            vmem((32, K), F32),
            vmem((8, K), F32),
            vmem((8, K), F32),
            vmem((2, 512, 512), F32),
            vmem((2, 2048, 512), BF16),
            vmem((2, 2048, 512), BF16),
            vmem((4, 2, 256, 128), F32),
            vmem((4, 256, 128), F32),
            vmem((4, 16, 16, 128), F32),
            vmem((4, 16, 16, 128), F32),
            vmem((64, 1024), F32),
            vmem((4, 4, 64, 256), F32),
            vmem((4, 4, 64, 256), F32),
            vmem((4, 4, 64, 256), F32),
            vmem((4, 3, 64, 256), F32),
            vmem((3, 4, 4, 256), F32),
            vmem((2, 4, 4, 256), F32),
            dma((1,)), dma((4,)), dma((4,)), dma((4,)), dma((1,)), dma((4,)),
            dma((4,)), dma((4,)), dma((4, 3)), dma((4, 3)), dma((2,)), dma((2,)), dma((2,)),
        ],
        compiler_params=pltpu.CompilerParams(
            collective_id=0, has_side_effects=True, vmem_limit_bytes=56 * 2**20
        ),
    )(
        jnp.swapaxes(spectra, 2, 3),
        dispersion.reshape(1, K),
        window_start,
        window_width,
        pupil,
    )
    return focused[None]


def solution(mesh):
    in_specs = (P(None, None, "pix", "spec"), P(), P(), P(), P(None, None, "pix"))
    out_specs = P("spec", None, "pix")
    return jax.shard_map(local, mesh=mesh, in_specs=in_specs, out_specs=out_specs, check_vma=False)
```

profile of v0, /device:TPU:1, one launch (start us, length us, event | category | flops | bytes accessed | tf_op | source)
XLA Modules:
  0.0 117.7 jit_solution(7505802188208133954)
XLA Ops:
  0.0 116.4 %shard_map.55 = f32[16,256]{1,0:T(8,128)} custom-call(f32[2,16,64,512]{3,2,1,0:T(8,128)} %bitcast.3, f32[1,2048]{1,0:T(1,128)} %bitcast.5, s32[32]{0:T(128)} %start.1, s32[32]{0:T(128)} %width.1, f32[2,2048,512]{2,1,0:T(8,128)} %pupil.1), custom_call_target="tpu_custom_call" | custom-call | tf_op jit(solution)/shard_map/pallas_call | solution.py:309
  116.4 1.3 %copy.7 = f32[1,16,256]{2,1,0:T(8,128)} copy(f32[1,16,256]{2,1,0:T(8,128)} %bitcast.4) | data formatting | bytes 32768
where the time goes:
time: 119 us; the launch traced here: 118 us
  Pallas kernels  116 us (97%)
  local copies, waits for them, and re-layouts  1.32 us (1%)
    pallas_call x1, Pallas kernels, local(): pl.pallas_call(kernel, out_shape=jax.ShapeDtypeStruct((16, 256), F32), in...  116 us

commit v1 on v0

v1 whole, which is shorter than its diff:
```python
import math

import jax
import jax.numpy as jnp
from jax import lax
from jax.experimental import pallas as pl
from jax.experimental.pallas import tpu as pltpu
from jax.sharding import PartitionSpec as P

K = 2048
MESH = pl.DeviceIdType.MESH
F32 = jnp.float32
BF16 = jnp.bfloat16
ROUNDS = 8
STEP = 2.0 * math.pi / K
NT = (((1,), (1,)), ((), ()))


def split(values):
    high = values.astype(BF16)
    return high, (values - high.astype(F32)).astype(BF16)


def kernel(
    spectra, disp, start, width, pupil, out,
    staged, packed, xbuf, xhl, th, tl, cosa, sina, cosb, sinb, pstage, ph, plo,
    part, zrecv, gsend, grecv, abuf, csend, own, crecv, frecv, hsend, hrecv,
    ls, xs, xr, zs, zr, gs, gr, cs, cr, fs, fr, hs, hr, ps,
):
    s = lax.axis_index("spec")
    p = lax.axis_index("pix")
    me = s // 2
    zh = s % 2
    y = me // 4
    x = me % 4
    zl = p // 2
    co = p % 2
    partner = {"spec": s + 1 - 2 * zh}
    sibling = {"pix": zl * 2 + 1 - co}
    before = {"spec": (s + 31) % 32}
    after = {"spec": (s + 1) % 32}

    def peer(t):
        return ((y + t // 4) % 4) * 4 + (x + t % 4) % 4

    def along(dz):
        return (zl + dz) % 4

    barrier = pltpu.get_barrier_semaphore()

    def greet(t, carry):
        pl.semaphore_signal(
            barrier, inc=1, device_id={"spec": peer(t) * 2 + zh}, device_id_type=MESH
        )
        return carry

    lax.fori_loop(1, 16, greet, 0)
    for device in (partner, sibling, before, after):
        pl.semaphore_signal(barrier, inc=1, device_id=device, device_id_type=MESH)
    for dz in (1, 2, 3):
        pl.semaphore_signal(
            barrier, inc=1, device_id={"pix": along(dz) * 2 + co}, device_id_type=MESH
        )
    left = lax.broadcasted_iota(jnp.int32, (64, 128), 1) < 64
    left8 = lax.broadcasted_iota(jnp.int32, (8, 128), 1) < 64

    def load(r):
        return pltpu.make_async_copy(spectra.at[:, pl.ds(r * 2, 2)], staged.at[r], ls.at[r])

    def pack(r):
        load(r).wait()
        for i in range(2):
            for m in range(4):
                at = slice(m * 128, m * 128 + 128)
                real = staged[r, 0, i, :, at]
                imag = staged[r, 1, i, :, at]
                packed[r, i * 8 + m * 2] = jnp.where(left, real, pltpu.roll(imag, 64, 1))
                packed[r, i * 8 + m * 2 + 1] = jnp.where(left, pltpu.roll(real, 64, 1), imag)

    def send_blocks(r):
        def send(t, carry):
            j = peer(t)
            pltpu.make_async_remote_copy(
                src_ref=packed.at[r, j], dst_ref=xbuf.at[r, me], send_sem=xs.at[0],
                recv_sem=xr.at[r], device_id={"spec": j * 2 + zh}, device_id_type=MESH,
            ).start()
            return carry

        lax.fori_loop(1, 16, send, 0)
        pltpu.make_async_copy(packed.at[r, me], xbuf.at[r, me], xr.at[r]).start()

    for r in range(ROUNDS):
        load(r).start()
    pack(0)
    pl.semaphore_wait(barrier, 22)
    send_blocks(0)
    pack(1)
    send_blocks(1)

    def fetch(n, slot):
        return pltpu.make_async_copy(
            pupil.at[n // 4, pl.ds((n % 4) * 512, 512)], pstage.at[slot], ps.at[slot]
        )

    fetch(0, 0).start()

    HALF = K // 2
    lane = lax.broadcasted_iota(jnp.int32, (8, HALF), 1)
    wave = (lane // 64) * 128 + zh * 64 + lane % 64
    pieces = []
    for m in range(8):
        a = jnp.broadcast_to(disp[:, m * 256 : m * 256 + 128], (8, 128))
        b = jnp.broadcast_to(disp[:, m * 256 + 128 : m * 256 + 256], (8, 128))
        lower = jnp.where(left8, a, pltpu.roll(b, 64, 1))
        upper = jnp.where(left8, pltpu.roll(a, 64, 1), b)
        pieces.append(jnp.where(zh == 0, lower, upper))
    phase = jnp.concatenate(pieces, axis=1)
    fine = lax.broadcasted_iota(jnp.int32, (8, HALF), 0)
    beta = STEP * ((fine * wave) & (K - 1)).astype(F32) + phase
    scale = 1.0 / math.sqrt(K)
    cosb[...] = jnp.cos(beta) * scale
    sinb[...] = jnp.sin(beta) * scale

    def coarse(n, carry):
        row = lax.broadcasted_iota(jnp.int32, (8, HALF), 0) + n * 8
        zg = jnp.where(row < 16, 1 - zh, zh)
        q = (row % 16) * 2 + zg
        alpha = STEP * ((8 * q * wave) & (K - 1)).astype(F32)
        cosa[pl.ds(pl.multiple_of(n * 8, 8), 8), :] = jnp.cos(alpha)
        sina[pl.ds(pl.multiple_of(n * 8, 8), 8), :] = jnp.sin(alpha)
        return carry

    lax.fori_loop(0, 4, coarse, 0)

    def rows(n, carry):
        ca = cosa[pl.ds(n, 1), :]
        sa = sina[pl.ds(n, 1), :]
        real = ca * cosb[...] - sa * sinb[...]
        imag = -(sa * cosb[...] + ca * sinb[...])
        high, low = split(jnp.concatenate([real, imag], axis=0))
        at = pl.ds(pl.multiple_of(n * 16, 16), 16)
        th[at, :] = high
        tl[at, :] = low
        return carry

    lax.fori_loop(0, 32, rows, 0)

    def convert(n, carry):
        slot = n % 2

        @pl.when(n < 7)
        def _():
            fetch(n + 1, 1 - slot).start()

        fetch(n, slot).wait()

        def piece(m, inner):
            high, low = split(pstage[slot, pl.ds(pl.multiple_of(m * 64, 64), 64), :])
            at = pl.ds(pl.multiple_of((n % 4) * 512 + m * 64, 64), 64)
            ph[n // 4, at, :] = high
            plo[n // 4, at, :] = low
            return inner

        lax.fori_loop(0, 8, piece, 0)
        return carry

    def convert_some(first, last):
        lax.fori_loop(first, last, convert, 0)

    convert_some(0, 4)

    def await_all(ref, sem):
        pltpu.make_async_copy(ref, ref, sem).wait()

    def half_copy(r, k):
        return pltpu.make_async_remote_copy(
            src_ref=part.at[r, k], dst_ref=zrecv.at[r, k], send_sem=zs.at[r, k],
            recv_sem=zr.at[r, k], device_id=partner, device_id_type=MESH,
        )

    def core_copy(r, k):
        return pltpu.make_async_remote_copy(
            src_ref=csend.at[r, k], dst_ref=crecv.at[r, k], send_sem=cs.at[r, k],
            recv_sem=cr.at[r, k], device_id=sibling, device_id_type=MESH,
        )

    def along_copy(r, k):
        return pltpu.make_async_remote_copy(
            src_ref=own.at[r, k], dst_ref=frecv.at[r, k], send_sem=fs.at[r, k],
            recv_sem=fr.at[r, k], device_id={"pix": along(k + 1) * 2 + co}, device_id_type=MESH,
        )

    def transform(r):
        await_all(xbuf.at[r], xr.at[r])

        def piece(n, carry):
            high, low = split(xbuf[r, pl.ds(n * 2, 2)].reshape(128, 128))
            at = pl.ds(pl.multiple_of(n * 128, 128), 128)
            xhl[at, 0:128] = high
            xhl[at, 128:256] = low
            return carry

        lax.fori_loop(0, 8, piece, 0)
        for half in (0, 1):
            at = slice(half * 256, half * 256 + 256)
            both = jnp.dot(th[at, :], xhl[...], preferred_element_type=F32)
            rest = jnp.dot(tl[at, :], xhl[:, 0:128], preferred_element_type=F32)
            done = (both[:, 0:128] + (both[:, 128:256] + rest)).reshape(16, 2, 8, 128)
            straight = done[:, 0].reshape(128, 128)
            crossed = pltpu.roll(done[:, 1].reshape(128, 128), 64, 1)
            left128 = lax.broadcasted_iota(jnp.int32, (128, 128), 1) < 64
            field = straight + jnp.where(left128, -crossed, crossed)
            part[r, half * 2] = field[0:64]
            part[r, half * 2 + 1] = field[64:128]
            if half == 0:
                half_copy(r, 0).start()
                half_copy(r, 1).start()

    def hand_out(r):
        def send(j):
            @pl.when(j != me)
            def _():
                pltpu.make_async_remote_copy(
                    src_ref=gsend.at[r, j], dst_ref=grecv.at[r, me], send_sem=gs.at[0],
                    recv_sem=gr.at[r], device_id={"spec": j * 2 + zh}, device_id_type=MESH,
                ).start()

        def ordered(t, carry):
            send(carry + ((t + me) % 8))
            return carry

        for k in (0, 1):
            half_copy(r, k).wait_recv()
            gsend[r, pl.ds(k * 8, 8)] = (part[r, 2 + k] + zrecv[r, k]).reshape(8, 8, 128)
            lax.fori_loop(0, 8, ordered, k * 8)
        pltpu.make_async_copy(gsend.at[r, me], grecv.at[r, me], gr.at[r]).start()

    def project(r):
        await_all(grecv.at[r], gr.at[r])
        for i in range(2):
            for m in range(4):
                a = grecv[r, i * 8 + m * 2]
                b = grecv[r, i * 8 + m * 2 + 1]
                real = jnp.where(left8, a, pltpu.roll(b, 64, 1))
                imag = jnp.where(left8, pltpu.roll(a, 64, 1), b)
                row = i * 8
                col = m * 128
                abuf[row : row + 8, col : col + 128] = real
                abuf[row : row + 8, 512 + col : 640 + col] = -imag
                abuf[16 + row : 24 + row, col : col + 128] = imag
                abuf[16 + row : 24 + row, 512 + col : 640 + col] = real
        high, low = split(abuf[...])
        stack = jnp.concatenate([high, low], axis=0)

        def product(b, core):
            at = pl.ds(pl.multiple_of((b * 2 + core) * 256, 256), 256)
            both = lax.dot_general(
                stack[:, 0:512], ph[0, at, :], NT, preferred_element_type=F32
            ) + lax.dot_general(stack[:, 512:1024], ph[1, at, :], NT, preferred_element_type=F32)
            rest = lax.dot_general(
                high[:, 0:512], plo[0, at, :], NT, preferred_element_type=F32
            ) + lax.dot_general(high[:, 512:1024], plo[1, at, :], NT, preferred_element_type=F32)
            return both[0:32] + (both[32:64] + rest)

        def give(k, carry):
            csend[r, k] = product(along(k + 1), 1 - co)
            core_copy(r, k).start()
            return carry

        lax.fori_loop(0, 4, give, 0)

        def pass_on(k, carry):
            mine = product(along(k + 1), co)
            core_copy(r, k).wait_recv()
            own[r, k] = mine + crecv[r, k]

            @pl.when(k < 3)
            def _():
                along_copy(r, k).start()

            return carry

        lax.fori_loop(0, 4, pass_on, 0)

    gate = s * 8 + lax.broadcasted_iota(jnp.int32, (8, 256), 0)

    def weight(owner):
        first = start[owner]
        return ((gate >= first) & (gate < first + width[owner])).astype(F32)

    def finish(r):
        for k in range(3):
            along_copy(r, k).wait_recv()
        total = own[r, 3] + (frecv[r, 0] + (frecv[r, 1] + frecv[r, 2]))
        power = total[0:16] * total[0:16] + total[16:32] * total[16:32]
        for n, owner in enumerate((s, (s + 31) % 32, (s + 1) % 32)):
            w = weight(owner)
            for i in range(2):
                hsend[n, r, i : i + 1, :] = jnp.sum(
                    power[i * 8 : i * 8 + 8] * w, axis=0, keepdims=True
                )

    def turn(n, carry):
        pl.when(n < 8)(lambda: transform(n))
        pl.when(n < 6)(lambda: pack(n + 2))
        pl.when((n >= 1) & (n < 9))(lambda: hand_out(n - 1))
        pl.when(n < 6)(lambda: send_blocks(n + 2))
        pl.when(n == 0)(lambda: convert_some(4, 8))
        pl.when((n >= 2) & (n < 10))(lambda: project(n - 2))
        pl.when(n >= 3)(lambda: finish(n - 3))
        return carry

    lax.fori_loop(0, ROUNDS + 3, turn, 0)

    copies = []
    for n, device in ((1, before), (2, after)):
        copy = pltpu.make_async_remote_copy(
            src_ref=hsend.at[n], dst_ref=hrecv.at[n - 1], send_sem=hs.at[n - 1],
            recv_sem=hr.at[n - 1], device_id=device, device_id_type=MESH,
        )
        copy.start()
        copies.append(copy)

    def sent(r, carry):
        await_all(xbuf.at[r, pl.ds(0, 15)], xs.at[0])
        await_all(gsend.at[r, pl.ds(0, 15)], gs.at[0])
        for k in range(2):
            half_copy(r, k).wait_send()
        for k in range(4):
            core_copy(r, k).wait_send()
        for k in range(3):
            along_copy(r, k).wait_send()
        return carry

    lax.fori_loop(0, ROUNDS, sent, 0)
    for copy in copies:
        copy.wait()
    for r in range(ROUNDS):
        out[r * 2 : r * 2 + 2, :] = hsend[0, r] + (hrecv[0, r] + hrecv[1, r])


def local(spectra, dispersion, window_start, window_width, pupil):
    vmem = pltpu.VMEM
    dma = pltpu.SemaphoreType.DMA
    hbm = pl.BlockSpec(memory_space=pl.ANY)
    smem = pl.BlockSpec(memory_space=pltpu.SMEM)
    focused = pl.pallas_call(
        kernel,
        out_shape=jax.ShapeDtypeStruct((16, 256), F32),
        in_specs=[hbm, pl.BlockSpec(memory_space=pltpu.VMEM), smem, smem, hbm],
        out_specs=pl.BlockSpec(memory_space=pltpu.VMEM),
        scratch_shapes=[
            vmem((8, 2, 2, 64, 512), F32),
            vmem((8, 16, 64, 128), F32),
            vmem((8, 16, 64, 128), F32),
            vmem((K // 2, 256), BF16),
            vmem((512, K // 2), BF16),
            vmem((512, K // 2), BF16),
            vmem((32, K // 2), F32),
            vmem((32, K // 2), F32),
            vmem((8, K // 2), F32),
            vmem((8, K // 2), F32),
            vmem((2, 512, 512), F32),
            vmem((2, 2048, 512), BF16),
            vmem((2, 2048, 512), BF16),
            vmem((8, 4, 64, 128), F32),
            vmem((8, 2, 64, 128), F32),
            vmem((8, 16, 8, 128), F32),
            vmem((8, 16, 8, 128), F32),
            vmem((32, 1024), F32),
            vmem((8, 4, 32, 256), F32),
            vmem((8, 4, 32, 256), F32),
            vmem((8, 4, 32, 256), F32),
            vmem((8, 3, 32, 256), F32),
            vmem((3, 8, 2, 256), F32),
            vmem((2, 8, 2, 256), F32),
            dma((8,)), dma((1,)), dma((8,)), dma((8, 2)), dma((8, 2)), dma((1,)), dma((8,)),
            dma((8, 4)), dma((8, 4)), dma((8, 3)), dma((8, 3)), dma((2,)), dma((2,)), dma((2,)),
        ],
        compiler_params=pltpu.CompilerParams(
            collective_id=0, has_side_effects=True, vmem_limit_bytes=56 * 2**20
        ),
    )(
        jnp.swapaxes(spectra, 2, 3),
        dispersion.reshape(1, K),
        window_start,
        window_width,
        pupil,
    )
    return focused[None]


def solution(mesh):
    in_specs = (P(None, None, "pix", "spec"), P(), P(), P(), P(None, None, "pix"))
    out_specs = P("spec", None, "pix")
    return jax.shard_map(local, mesh=mesh, in_specs=in_specs, out_specs=out_specs, check_vma=False)
```

time: 119 us -> 92.7 us (0.78)
  Pallas kernels: 116 us -> 91.1 us
    pallas_call x1, Pallas kernels: 116 us -> 91.1 us  [local(): pl.pallas_call(kernel, out_shape=jax.ShapeDtypeStruct((16, 256), F32), in...]
where the time goes in v1:
time: 92.7 us; the launch traced here: 92.4 us
  Pallas kernels  91.1 us (98%)
  local copies, waits for them, and re-layouts  1.32 us (1%)
    pallas_call x1, Pallas kernels, local(): pl.pallas_call(kernel, out_shape=jax.ShapeDtypeStruct((16, 256), F32), in...  91.1 us

profile of v1, /device:TPU:1, one launch (start us, length us, event | category | flops | bytes accessed | tf_op | source)
XLA Modules:
  0.0 92.4 jit_solution(6513054725037510885)
XLA Ops:
  0.0 91.1 %shard_map.55 = f32[16,256]{1,0:T(8,128)} custom-call(f32[2,16,64,512]{3,2,1,0:T(8,128)} %bitcast.3, f32[1,2048]{1,0:T(1,128)} %bitcast.5, s32[32]{0:T(128)} %start.1, s32[32]{0:T(128)} %width.1, f32[2,2048,512]{2,1,0:T(8,128)} %pupil.1), custom_call_target="tpu_custom_call" | custom-call | tf_op jit(solution)/shard_map/pallas_call | solution.py:347
  91.1 1.3 %copy.7 = f32[1,16,256]{2,1,0:T(8,128)} copy(f32[1,16,256]{2,1,0:T(8,128)} %bitcast.4) | data formatting | bytes 32768

commit v2 on v1

--- a/solution.py
+++ b/solution.py
@@ -13,7 +13,8 @@
 BF16 = jnp.bfloat16
 ROUNDS = 8
 STEP = 2.0 * math.pi / K
-NT = (((1,), (1,)), ((), ()))
+LAST = ROUNDS - 1
+SPLIT = 16
 
 
 def split(values):
@@ -24,8 +25,8 @@
 def kernel(
     spectra, disp, start, width, pupil, out,
     staged, packed, xbuf, xhl, th, tl, cosa, sina, cosb, sinb, pstage, ph, plo,
-    part, zrecv, gsend, grecv, abuf, csend, own, crecv, frecv, hsend, hrecv,
-    ls, xs, xr, zs, zr, gs, gr, cs, cr, fs, fr, hs, hr, ps,
+    part, zrecv, gsend, grecv, glast, abuf, csend, own, crecv, frecv, hsend, hrecv,
+    ls, xs, xr, zs, zr, gs, gr, cs, cr, fs, fr, hs, hr, ps, lsend, lr,
 ):
     s = lax.axis_index("spec")
     p = lax.axis_index("pix")
@@ -77,7 +78,7 @@
                 packed[r, i * 8 + m * 2] = jnp.where(left, real, pltpu.roll(imag, 64, 1))
                 packed[r, i * 8 + m * 2 + 1] = jnp.where(left, pltpu.roll(real, 64, 1), imag)
 
-    def send_blocks(r):
+    def send_blocks(r, first, last):
         def send(t, carry):
             j = peer(t)
             pltpu.make_async_remote_copy(
@@ -86,16 +87,20 @@
             ).start()
             return carry
 
-        lax.fori_loop(1, 16, send, 0)
+        lax.fori_loop(first, last, send, 0)
+
+    def keep_block(r):
         pltpu.make_async_copy(packed.at[r, me], xbuf.at[r, me], xr.at[r]).start()
 
     for r in range(ROUNDS):
         load(r).start()
     pack(0)
     pl.semaphore_wait(barrier, 22)
-    send_blocks(0)
+    send_blocks(0, 1, 16)
+    keep_block(0)
     pack(1)
-    send_blocks(1)
+    send_blocks(1, 1, SPLIT)
+    keep_block(1)
 
     def fetch(n, slot):
         return pltpu.make_async_copy(
@@ -155,19 +160,20 @@
         fetch(n, slot).wait()
 
         def piece(m, inner):
-            high, low = split(pstage[slot, pl.ds(pl.multiple_of(m * 64, 64), 64), :])
-            at = pl.ds(pl.multiple_of((n % 4) * 512 + m * 64, 64), 64)
-            ph[n // 4, at, :] = high
-            plo[n // 4, at, :] = low
+            rows_at = pl.ds(pl.multiple_of(m * 128, 128), 128)
+            high, low = split(pstage[slot, rows_at, :].T)
+            at = pl.ds(pl.multiple_of((n % 4) * 512 + m * 128, 128), 128)
+            ph[n // 4, :, at] = high
+            plo[n // 4, :, at] = low
             return inner
 
-        lax.fori_loop(0, 8, piece, 0)
+        lax.fori_loop(0, 4, piece, 0)
         return carry
 
     def convert_some(first, last):
         lax.fori_loop(first, last, convert, 0)
 
-    convert_some(0, 4)
+    convert_some(0, 3)
 
     def await_all(ref, sem):
         pltpu.make_async_copy(ref, ref, sem).wait()
@@ -189,6 +195,26 @@
             src_ref=own.at[r, k], dst_ref=frecv.at[r, k], send_sem=fs.at[r, k],
             recv_sem=fr.at[r, k], device_id={"pix": along(k + 1) * 2 + co}, device_id_type=MESH,
         )
+
+    def gates(half, j):
+        at = pl.ds(pl.multiple_of((j % 8) * 8, 8), 8)
+        return part.at[LAST, half * 2 + j // 8, at]
+
+    def across(t, carry):
+        j = peer(t)
+        pltpu.make_async_remote_copy(
+            src_ref=gates(0, j), dst_ref=glast.at[0, me], send_sem=lsend.at[0],
+            recv_sem=lr.at[0], device_id={"spec": j * 2 + 1 - zh}, device_id_type=MESH,
+        ).start()
+        return carry
+
+    def within(t, carry):
+        j = peer(t)
+        pltpu.make_async_remote_copy(
+            src_ref=gates(1, j), dst_ref=glast.at[1, me], send_sem=lsend.at[1],
+            recv_sem=lr.at[1], device_id={"spec": j * 2 + zh}, device_id_type=MESH,
+        ).start()
+        return carry
 
     def transform(r):
         await_all(xbuf.at[r], xr.at[r])
@@ -213,8 +239,20 @@
             part[r, half * 2] = field[0:64]
             part[r, half * 2 + 1] = field[64:128]
             if half == 0:
-                half_copy(r, 0).start()
-                half_copy(r, 1).start()
+                @pl.when(r < LAST)
+                def _():
+                    half_copy(r, 0).start()
+                    half_copy(r, 1).start()
+
+                @pl.when(r == LAST)
+                def _():
+                    lax.fori_loop(0, 16, across, 0)
+
+            else:
+                @pl.when(r == LAST)
+                def _():
+                    lax.fori_loop(1, 16, within, 0)
+                    pltpu.make_async_copy(gates(1, me), glast.at[1, me], lr.at[1]).start()
 
     def hand_out(r):
         def send(j):
@@ -235,52 +273,81 @@
             lax.fori_loop(0, 8, ordered, k * 8)
         pltpu.make_async_copy(gsend.at[r, me], grecv.at[r, me], gr.at[r]).start()
 
-    def project(r):
-        await_all(grecv.at[r], gr.at[r])
+    def collect(r, q):
         for i in range(2):
             for m in range(4):
                 a = grecv[r, i * 8 + m * 2]
                 b = grecv[r, i * 8 + m * 2 + 1]
                 real = jnp.where(left8, a, pltpu.roll(b, 64, 1))
                 imag = jnp.where(left8, pltpu.roll(a, 64, 1), b)
-                row = i * 8
+                row = q * 32 + i * 8
                 col = m * 128
                 abuf[row : row + 8, col : col + 128] = real
                 abuf[row : row + 8, 512 + col : 640 + col] = -imag
                 abuf[16 + row : 24 + row, col : col + 128] = imag
                 abuf[16 + row : 24 + row, 512 + col : 640 + col] = real
-        high, low = split(abuf[...])
+
+    def project(r, count):
+        for q in range(count):
+            collect(r + q, q)
+        size = count * 32
+        high, low = split(abuf[0:size, :])
         stack = jnp.concatenate([high, low], axis=0)
 
         def product(b, core):
             at = pl.ds(pl.multiple_of((b * 2 + core) * 256, 256), 256)
-            both = lax.dot_general(
-                stack[:, 0:512], ph[0, at, :], NT, preferred_element_type=F32
-            ) + lax.dot_general(stack[:, 512:1024], ph[1, at, :], NT, preferred_element_type=F32)
-            rest = lax.dot_general(
-                high[:, 0:512], plo[0, at, :], NT, preferred_element_type=F32
-            ) + lax.dot_general(high[:, 512:1024], plo[1, at, :], NT, preferred_element_type=F32)
-            return both[0:32] + (both[32:64] + rest)
-
-        def give(k, carry):
-            csend[r, k] = product(along(k + 1), 1 - co)
-            core_copy(r, k).start()
+            both = jnp.dot(stack[:, 0:512], ph[0, :, at], preferred_element_type=F32) + jnp.dot(
+                stack[:, 512:1024], ph[1, :, at], preferred_element_type=F32
+            )
+            rest = jnp.dot(high[:, 0:512], plo[0, :, at], preferred_element_type=F32) + jnp.dot(
+                high[:, 512:1024], plo[1, :, at], preferred_element_type=F32
+            )
+            return both[0:size] + (both[size : 2 * size] + rest)
+
+        def give(k):
+            values = product(along(k + 1), 1 - co)
+            for q in range(count):
+                csend[r + q, k] = values[q * 32 : q * 32 + 32]
+                core_copy(r + q, k).start()
+
+        def first(k, carry):
+            give(k)
             return carry
 
-        lax.fori_loop(0, 4, give, 0)
-
-        def pass_on(k, carry):
+        lax.fori_loop(0, 4, first, 0)
+
+        def step(k, carry):
             mine = product(along(k + 1), co)
-            core_copy(r, k).wait_recv()
-            own[r, k] = mine + crecv[r, k]
+            for q in range(count):
+                core_copy(r + q, k).wait_recv()
+                own[r + q, k] = mine[q * 32 : q * 32 + 32] + crecv[r + q, k]
 
             @pl.when(k < 3)
             def _():
-                along_copy(r, k).start()
+                for q in range(count):
+                    along_copy(r + q, k).start()
 
             return carry
 
-        lax.fori_loop(0, 4, pass_on, 0)
+        lax.fori_loop(0, 4, step, 0)
+
+    def project_one(r):
+        @pl.when(r < LAST)
+        def _():
+            await_all(grecv.at[r], gr.at[r])
+
+        @pl.when(r == LAST)
+        def _():
+            await_all(glast.at[0], lr.at[0])
+            await_all(glast.at[1], lr.at[1])
+            grecv[r] = glast[0] + glast[1]
+
+        project(r, 1)
+
+    def project_two(r):
+        for q in range(2):
+            await_all(grecv.at[r + q], gr.at[r + q])
+        project(r, 2)
 
     gate = s * 8 + lax.broadcasted_iota(jnp.int32, (8, 256), 0)
 
@@ -302,15 +369,24 @@
 
     def turn(n, carry):
         pl.when(n < 8)(lambda: transform(n))
-        pl.when(n < 6)(lambda: pack(n + 2))
-        pl.when((n >= 1) & (n < 9))(lambda: hand_out(n - 1))
-        pl.when(n < 6)(lambda: send_blocks(n + 2))
-        pl.when(n == 0)(lambda: convert_some(4, 8))
-        pl.when((n >= 2) & (n < 10))(lambda: project(n - 2))
-        pl.when(n >= 3)(lambda: finish(n - 3))
-        return carry
-
-    lax.fori_loop(0, ROUNDS + 3, turn, 0)
+        pl.when((n >= 1) & (n < 8))(lambda: hand_out(n - 1))
+        pl.when(n < 7)(lambda: send_blocks(n + 1, SPLIT, 16))
+
+        @pl.when(n < 6)
+        def _():
+            pack(n + 2)
+            send_blocks(n + 2, 1, SPLIT)
+            keep_block(n + 2)
+
+        pl.when(n == 0)(lambda: convert_some(3, 6))
+        pl.when(n == 1)(lambda: convert_some(6, 8))
+        pl.when(n >= 2)(lambda: project_one(n - 2))
+        pl.when((n >= 3) & (n < 9))(lambda: finish(n - 3))
+        return carry
+
+    lax.fori_loop(0, ROUNDS + 2, turn, 0)
+    finish(6)
+    finish(7)
 
     copies = []
     for n, device in ((1, before), (2, after)):
@@ -323,9 +399,13 @@
 
     def sent(r, carry):
         await_all(xbuf.at[r, pl.ds(0, 15)], xs.at[0])
-        await_all(gsend.at[r, pl.ds(0, 15)], gs.at[0])
-        for k in range(2):
-            half_copy(r, k).wait_send()
+
+        @pl.when(r < LAST)
+        def _():
+            await_all(gsend.at[r, pl.ds(0, 15)], gs.at[0])
+            for k in range(2):
+                half_copy(r, k).wait_send()
+
         for k in range(4):
             core_copy(r, k).wait_send()
         for k in range(3):
@@ -333,6 +413,8 @@
         return carry
 
     lax.fori_loop(0, ROUNDS, sent, 0)
+    await_all(glast.at[0], lsend.at[0])
+    await_all(glast.at[1, pl.ds(0, 15)], lsend.at[1])
     for copy in copies:
         copy.wait()
     for r in range(ROUNDS):
@@ -361,13 +443,14 @@
             vmem((8, K // 2), F32),
             vmem((8, K // 2), F32),
             vmem((2, 512, 512), F32),
-            vmem((2, 2048, 512), BF16),
-            vmem((2, 2048, 512), BF16),
+            vmem((2, 512, 2048), BF16),
+            vmem((2, 512, 2048), BF16),
             vmem((8, 4, 64, 128), F32),
             vmem((8, 2, 64, 128), F32),
             vmem((8, 16, 8, 128), F32),
             vmem((8, 16, 8, 128), F32),
-            vmem((32, 1024), F32),
+            vmem((2, 16, 8, 128), F32),
+            vmem((64, 1024), F32),
             vmem((8, 4, 32, 256), F32),
             vmem((8, 4, 32, 256), F32),
             vmem((8, 4, 32, 256), F32),
@@ -375,7 +458,7 @@
             vmem((3, 8, 2, 256), F32),
             vmem((2, 8, 2, 256), F32),
             dma((8,)), dma((1,)), dma((8,)), dma((8, 2)), dma((8, 2)), dma((1,)), dma((8,)),
-            dma((8, 4)), dma((8, 4)), dma((8, 3)), dma((8, 3)), dma((2,)), dma((2,)), dma((2,)),
+            dma((8, 4)), dma((8, 4)), dma((8, 3)), dma((8, 3)), dma((2,)), dma((2,)), dma((2,)), dma((2,)), dma((2,)),
         ],
         compiler_params=pltpu.CompilerParams(
             collective_id=0, has_side_effects=True, vmem_limit_bytes=56 * 2**20

time: 92.7 us -> 91.1 us (0.983)
  Pallas kernels: 91.1 us -> 89.4 us
    pallas_call x1, Pallas kernels: 91.1 us -> 89.4 us  [local(): pl.pallas_call(kernel, out_shape=jax.ShapeDtypeStruct((16, 256), F32), in...]
where the time goes in v2:
time: 91.1 us; the launch traced here: 90.8 us
  Pallas kernels  89.4 us (98%)
  local copies, waits for them, and re-layouts  1.32 us (1%)
    pallas_call x1, Pallas kernels, local(): pl.pallas_call(kernel, out_shape=jax.ShapeDtypeStruct((16, 256), F32), in...  89.4 us

profile of v2, /device:TPU:1, one launch (start us, length us, event | category | flops | bytes accessed | tf_op | source)
XLA Modules:
  0.0 90.8 jit_solution(8509055241470927531)
XLA Ops:
  0.0 89.4 %shard_map.55 = f32[16,256]{1,0:T(8,128)} custom-call(f32[2,16,64,512]{3,2,1,0:T(8,128)} %bitcast.3, f32[1,2048]{1,0:T(1,128)} %bitcast.5, s32[32]{0:T(128)} %start.1, s32[32]{0:T(128)} %width.1, f32[2,2048,512]{2,1,0:T(8,128)} %pupil.1), custom_call_target="tpu_custom_call" | custom-call | tf_op jit(solution)/shard_map/pallas_call | solution.py:429
  89.4 1.3 %copy.7 = f32[1,16,256]{2,1,0:T(8,128)} copy(f32[1,16,256]{2,1,0:T(8,128)} %bitcast.4) | data formatting | bytes 32768

commit v3 on v2

--- a/solution.py
+++ b/solution.py
@@ -14,7 +14,13 @@
 ROUNDS = 8
 STEP = 2.0 * math.pi / K
 LAST = ROUNDS - 1
-SPLIT = 16
+
+
+def hops(t):
+    return min(t % 4, 4 - t % 4) + min(t // 4, 4 - t // 4)
+
+
+NEAR = sorted(range(1, 16), key=hops)
 
 
 def split(values):
@@ -78,16 +84,13 @@
                 packed[r, i * 8 + m * 2] = jnp.where(left, real, pltpu.roll(imag, 64, 1))
                 packed[r, i * 8 + m * 2 + 1] = jnp.where(left, pltpu.roll(real, 64, 1), imag)
 
-    def send_blocks(r, first, last):
-        def send(t, carry):
+    def send_blocks(r):
+        for t in NEAR:
             j = peer(t)
             pltpu.make_async_remote_copy(
                 src_ref=packed.at[r, j], dst_ref=xbuf.at[r, me], send_sem=xs.at[0],
                 recv_sem=xr.at[r], device_id={"spec": j * 2 + zh}, device_id_type=MESH,
             ).start()
-            return carry
-
-        lax.fori_loop(first, last, send, 0)
 
     def keep_block(r):
         pltpu.make_async_copy(packed.at[r, me], xbuf.at[r, me], xr.at[r]).start()
@@ -96,10 +99,10 @@
         load(r).start()
     pack(0)
     pl.semaphore_wait(barrier, 22)
-    send_blocks(0, 1, 16)
+    send_blocks(0)
     keep_block(0)
     pack(1)
-    send_blocks(1, 1, SPLIT)
+    send_blocks(1)
     keep_block(1)
 
     def fetch(n, slot):
@@ -178,10 +181,10 @@
     def await_all(ref, sem):
         pltpu.make_async_copy(ref, ref, sem).wait()
 
-    def half_copy(r, k):
+    def half_copy(r):
         return pltpu.make_async_remote_copy(
-            src_ref=part.at[r, k], dst_ref=zrecv.at[r, k], send_sem=zs.at[r, k],
-            recv_sem=zr.at[r, k], device_id=partner, device_id_type=MESH,
+            src_ref=part.at[r, pl.ds(0, 2)], dst_ref=zrecv.at[r], send_sem=zs.at[r],
+            recv_sem=zr.at[r], device_id=partner, device_id_type=MESH,
         )
 
     def core_copy(r, k):
@@ -241,8 +244,7 @@
             if half == 0:
                 @pl.when(r < LAST)
                 def _():
-                    half_copy(r, 0).start()
-                    half_copy(r, 1).start()
+                    half_copy(r).start()
 
                 @pl.when(r == LAST)
                 def _():
@@ -255,22 +257,14 @@
                     pltpu.make_async_copy(gates(1, me), glast.at[1, me], lr.at[1]).start()
 
     def hand_out(r):
-        def send(j):
-            @pl.when(j != me)
-            def _():
-                pltpu.make_async_remote_copy(
-                    src_ref=gsend.at[r, j], dst_ref=grecv.at[r, me], send_sem=gs.at[0],
-                    recv_sem=gr.at[r], device_id={"spec": j * 2 + zh}, device_id_type=MESH,
-                ).start()
-
-        def ordered(t, carry):
-            send(carry + ((t + me) % 8))
-            return carry
-
-        for k in (0, 1):
-            half_copy(r, k).wait_recv()
-            gsend[r, pl.ds(k * 8, 8)] = (part[r, 2 + k] + zrecv[r, k]).reshape(8, 8, 128)
-            lax.fori_loop(0, 8, ordered, k * 8)
+        half_copy(r).wait_recv()
+        gsend[r] = (part[r, 2:4] + zrecv[r]).reshape(16, 8, 128)
+        for t in NEAR:
+            j = peer(t)
+            pltpu.make_async_remote_copy(
+                src_ref=gsend.at[r, j], dst_ref=grecv.at[r, me], send_sem=gs.at[0],
+                recv_sem=gr.at[r], device_id={"spec": j * 2 + zh}, device_id_type=MESH,
+            ).start()
         pltpu.make_async_copy(gsend.at[r, me], grecv.at[r, me], gr.at[r]).start()
 
     def collect(r, q):
@@ -370,12 +364,11 @@
     def turn(n, carry):
         pl.when(n < 8)(lambda: transform(n))
         pl.when((n >= 1) & (n < 8))(lambda: hand_out(n - 1))
-        pl.when(n < 7)(lambda: send_blocks(n + 1, SPLIT, 16))
 
         @pl.when(n < 6)
         def _():
             pack(n + 2)
-            send_blocks(n + 2, 1, SPLIT)
+            send_blocks(n + 2)
             keep_block(n + 2)
 
         pl.when(n == 0)(lambda: convert_some(3, 6))
@@ -403,8 +396,7 @@
         @pl.when(r < LAST)
         def _():
             await_all(gsend.at[r, pl.ds(0, 15)], gs.at[0])
-            for k in range(2):
-                half_copy(r, k).wait_send()
+            half_copy(r).wait_send()
 
         for k in range(4):
             core_copy(r, k).wait_send()
@@ -457,7 +449,7 @@
             vmem((8, 3, 32, 256), F32),
             vmem((3, 8, 2, 256), F32),
             vmem((2, 8, 2, 256), F32),
-            dma((8,)), dma((1,)), dma((8,)), dma((8, 2)), dma((8, 2)), dma((1,)), dma((8,)),
+            dma((8,)), dma((1,)), dma((8,)), dma((8,)), dma((8,)), dma((1,)), dma((8,)),
             dma((8, 4)), dma((8, 4)), dma((8, 3)), dma((8, 3)), dma((2,)), dma((2,)), dma((2,)), dma((2,)), dma((2,)),
         ],
         compiler_params=pltpu.CompilerParams(

time: 91.1 us -> 90.9 us (level)
  no operation moved by 1% of the time
where the time goes in v3:
time: 90.9 us; the launch traced here: 90.7 us
  Pallas kernels  89.3 us (98%)
  local copies, waits for them, and re-layouts  1.32 us (1%)
    pallas_call x1, Pallas kernels, local(): pl.pallas_call(kernel, out_shape=jax.ShapeDtypeStruct((16, 256), F32), in...  89.3 us

profile of v3, /device:TPU:1, one launch (start us, length us, event | category | flops | bytes accessed | tf_op | source)
XLA Modules:
  0.0 90.7 jit_solution(15304341575547415555)
XLA Ops:
  0.0 89.3 %shard_map.55 = f32[16,256]{1,0:T(8,128)} custom-call(f32[2,16,64,512]{3,2,1,0:T(8,128)} %bitcast.3, f32[1,2048]{1,0:T(1,128)} %bitcast.5, s32[32]{0:T(128)} %start.1, s32[32]{0:T(128)} %width.1, f32[2,2048,512]{2,1,0:T(8,128)} %pupil.1), custom_call_target="tpu_custom_call" | custom-call | tf_op jit(solution)/shard_map/pallas_call | solution.py:421
  89.3 1.3 %copy.7 = f32[1,16,256]{2,1,0:T(8,128)} copy(f32[1,16,256]{2,1,0:T(8,128)} %bitcast.4) | data formatting | bytes 32768
